TPU v7x, 32 devices: a whole 2x2x4 slice. The times are simulated.
32 devices in a mesh: sector: 4 (over z), rows: 8 (over y, x, core).
Axes of the slice: x: 2, y: 2, z: 4, core: 2. Of those that a mesh axis runs over, the one named last changes fastest.
Arguments:
- x_block: bfloat16 [4, 10240, 300], P('sector', 'rows')
- h_diag: bfloat16 [4, 10240, 1280], P('sector', 'rows')
- h_right: bfloat16 [4, 10240, 1280], P('sector', 'rows')
- pattern: int32 [4, 2, 80, 10], P('sector', None, 'rows'), may hold values from 0 to 1, as said below
Outputs:
- q_block: bfloat16 [4, 10240, 300], P('sector', 'rows')
- hproj: float32 [4, 300, 300], P('sector')
- correlation: float32 [4, 300, 300], P('sector')
Inputs may be any that keep to these rules, and one draw needn't show every extreme that they name: Within each 1280 x 1280 tile, pattern[s, 0] is symmetric with ones on its diagonal; h_diag's tiles are symmetric.
All inputs are finite; a program needn't handle non-finite values.
Results may differ from a plain program's by a relative error of at most 0.011.
Values may be sent and summed in bfloat16 or wider, within the bound.
No kernel may reach another device: no remote copies, remote signals or barrier semaphores. Data moves between devices by JAX's collectives and lax.ppermute only.
A program may use at most 64 MiB of HBM per device.

v0:
```python
import functools

import jax
import jax.numpy as jnp
from jax import lax
from jax.experimental import pallas as pl
from jax.experimental.pallas import tpu as pltpu
from jax.sharding import PartitionSpec as P

SUBBLOCK = 128
LANES = 128
PANEL = 16
WHOLE = pl.BlockSpec(memory_space=pltpu.VMEM)
SCALARS = pl.BlockSpec(memory_space=pltpu.SMEM)
ANYWHERE = pl.BlockSpec(memory_space=pl.ANY)
MIB = 1024 * 1024
FIRST_STAGE_FLOPS = 2 * 10**9
LAST_STAGES_FLOPS = 4 * 10**9


def params(mib=48):
    return pltpu.CompilerParams(vmem_limit_bytes=mib * MIB)


def cost(flops, bytes_accessed):
    return pl.CostEstimate(flops=flops, bytes_accessed=bytes_accessed, transcendentals=0)


def round_up(value, step):
    return (value + step - 1) // step * step


def dot(left, right, dims, precision=None):
    return lax.dot_general(
        left, right, (dims, ((), ())), precision=precision, preferred_element_type=jnp.float32
    )


def block_mask(mask_ref, which, cols):
    blocks = mask_ref[:, which, :].astype(jnp.float32)
    col = lax.broadcasted_iota(jnp.int32, (blocks.shape[1], cols), 1)
    block = lax.broadcasted_iota(jnp.int32, (blocks.shape[1], cols), 0)
    return dot(blocks, jnp.where(col // SUBBLOCK == block, 1.0, 0.0), ((1,), (0,)))


def mask_rows(tile_ref, mask, start, size):
    cols = tile_ref.shape[1]
    for i in range(start // SUBBLOCK, (start + size) // SUBBLOCK):
        keep = jnp.broadcast_to(mask[i : i + 1, :], (PANEL, cols)).astype(tile_ref.dtype)
        for row in range(i * SUBBLOCK, (i + 1) * SUBBLOCK, PANEL):
            tile_ref[row : row + PANEL, :] = tile_ref[row : row + PANEL, :] * keep


def strips(rows, width):
    return [(start, min(width, rows - start)) for start in range(0, rows, width)]


def halves(rows):
    first = rows // 512 * 256
    return [(0, first), (first, rows - first)] if first else [(0, rows)]


def copies_of(source, target, sems):
    copies = []
    for n, (start, size) in enumerate(halves(target.shape[0])):
        here = (pl.ds(start, size), slice(None))
        copies.append(pltpu.make_async_copy(source.at[here], target.at[here], sems.at[n]))
    return copies


def product(x_ref, tile_ref, copies, mask, sum_ref, out_ref):
    rows = tile_ref.shape[0]
    for n, (start, size) in enumerate(halves(rows)):
        copies[n].wait()
        mask_rows(tile_ref, mask, start, size)
        last = n + 1 == len(copies)
        for col, cols in strips(rows, 2 * SUBBLOCK):
            here = (slice(None), slice(col, col + cols))
            term = dot(
                x_ref[:, start : start + size],
                tile_ref[start : start + size, col : col + cols],
                ((1,), (0,)),
            )
            if n > 0:
                term = sum_ref[here] + term
            if last:
                out_ref[here] = term.astype(out_ref.dtype)
            else:
                sum_ref[here] = term


def tile_kernel(which, mask_ref, x_hbm, tile_hbm, out_ref, x_ref, tile_ref, sum_ref, x_sem, sems):
    rows = tile_ref.shape[0]
    copies = copies_of(tile_hbm, tile_ref, sems)
    copy_x = pltpu.make_async_copy(x_hbm, x_ref, x_sem)
    copy_x.start()
    for copy in copies:
        copy.start()
    mask = block_mask(mask_ref, which, rows)
    copy_x.wait()
    product(x_ref, tile_ref, copies, mask, sum_ref, out_ref)


def tile_product(which, masks, x_t, tile, dtype, mib):
    channels, rows = x_t.shape
    return pl.pallas_call(
        functools.partial(tile_kernel, which),
        in_specs=[WHOLE, ANYWHERE, ANYWHERE],
        out_specs=WHOLE,
        out_shape=jax.ShapeDtypeStruct((channels, rows), dtype),
        scratch_shapes=[
            pltpu.VMEM((channels, rows), x_t.dtype),
            pltpu.VMEM((rows, rows), tile.dtype),
            pltpu.VMEM((channels, rows), jnp.float32),
            pltpu.SemaphoreType.DMA,
            pltpu.SemaphoreType.DMA((2,)),
        ],
        compiler_params=params(mib),
        cost_estimate=cost(2 * channels * rows * rows, 2 * rows * rows),
    )(masks, x_t, tile)


def later_kernel(mask_ref, later_ref, tile_hbm, first_ref, out_ref, tile_ref, sems):
    rows = tile_ref.shape[0]
    copies = copies_of(tile_hbm, tile_ref, sems)
    for copy in copies:
        copy.start()
    mask = block_mask(mask_ref, 1, rows)
    for n, (start, size) in enumerate(halves(rows)):
        copies[n].wait()
        mask_rows(tile_ref, mask, start, size)
        for row, count in strips(size, 2 * SUBBLOCK):
            here = (slice(None), slice(start + row, start + row + count))
            out_ref[here] = first_ref[here] + dot(
                later_ref[...], tile_ref[start + row : start + row + count, :], ((1,), (1,))
            )


def later_product(masks, later, tile, first):
    channels, rows = later.shape
    return pl.pallas_call(
        later_kernel,
        in_specs=[WHOLE, WHOLE, ANYWHERE, WHOLE],
        out_specs=WHOLE,
        out_shape=jax.ShapeDtypeStruct((channels, rows), jnp.float32),
        scratch_shapes=[
            pltpu.VMEM((rows, rows), tile.dtype),
            pltpu.SemaphoreType.DMA((2,)),
        ],
        compiler_params=params(),
        cost_estimate=cost(2 * channels * rows * rows, 2 * rows * rows),
    )(masks, later, tile, first)


def lower_rows(channels):
    rows = round_up(channels, PANEL)
    return sum(rows - g * LANES for g in range(round_up(channels, LANES) // LANES))


def full_rows(channels):
    rows, wide = round_up(channels, PANEL), round_up(channels, LANES)
    whole = channels // LANES
    rest = rows - whole * LANES
    return round_up(whole * rows + rest * (wide // LANES), 4 * PANEL)


def store_padded(ref, value):
    size, tall = value.shape[0], ref.shape[0]
    start = size // PANEL * PANEL
    ref[start:tall, :] = jnp.zeros((tall - start, ref.shape[1]), ref.dtype)
    ref[0:size, :] = value


def lower_products(pad_ref, rows, out_ref):
    offset = 0
    for g in range(pad_ref.shape[0] // LANES):
        block = pad_ref[g * LANES : (g + 1) * LANES, :]
        out_ref[offset : offset + rows - g * LANES, :] = dot(
            pad_ref[g * LANES : rows, :], block, ((1,), (1,))
        )
        offset += rows - g * LANES


def full_products(left_ref, right_ref, channels, out_ref):
    rows, wide = round_up(channels, PANEL), round_up(channels, LANES)
    whole = channels // LANES
    for g in range(whole):
        out_ref[g * rows : (g + 1) * rows, :] = dot(
            left_ref[0:rows, :], right_ref[g * LANES : (g + 1) * LANES, :], ((1,), (1,))
        )
    rest = rows - whole * LANES
    for g in range(wide // LANES if rest else 0):
        out_ref[whole * rows + g * rest : whole * rows + (g + 1) * rest, :] = dot(
            right_ref[whole * LANES : rows, :],
            left_ref[g * LANES : (g + 1) * LANES, :],
            ((1,), (1,)),
        )
    used = whole * rows + rest * (wide // LANES)
    if used < out_ref.shape[0]:
        out_ref[used:, :] = jnp.zeros((out_ref.shape[0] - used, LANES), out_ref.dtype)


def full_matrix(pack_ref, channels):
    rows, wide = round_up(channels, PANEL), round_up(channels, LANES)
    whole = channels // LANES
    rest = rows - whole * LANES
    parts = [pack_ref[g * rows : (g + 1) * rows, :] for g in range(whole)]
    if rest:
        tail = jnp.concatenate(
            [
                pack_ref[whole * rows + g * rest : whole * rows + (g + 1) * rest, :]
                for g in range(wide // LANES)
            ],
            axis=1,
        )
        tail = jnp.concatenate([tail, jnp.zeros((LANES - rest, wide), tail.dtype)], axis=0)
        parts.append(tail.T[0:rows, :])
    return jnp.concatenate(parts, axis=1)


def cut(pack_ref, core, mine_ref, other_ref):
    half = mine_ref.shape[0]
    mine_ref[...] = pack_ref[pl.ds(pl.multiple_of(core * half, 8), half), :].astype(mine_ref.dtype)
    other_ref[...] = pack_ref[pl.ds(pl.multiple_of((1 - core) * half, 8), half), :].astype(
        other_ref.dtype
    )


def join(pack_ref, core, mine, other):
    half = mine.shape[0]
    pack_ref[pl.ds(pl.multiple_of(core * half, 8), half), :] = mine
    pack_ref[pl.ds(pl.multiple_of((1 - core) * half, 8), half), :] = other


def gram_kernel(core_ref, part_ref, carried_ref, y_ref, g_mine, g_other, pad_ref, gram_ref):
    image = (part_ref[...] + carried_ref[...].astype(jnp.float32)).astype(y_ref.dtype)
    y_ref[...] = image
    store_padded(pad_ref, image)
    lower_products(pad_ref, round_up(image.shape[0], PANEL), gram_ref)
    cut(gram_ref, core_ref[0], g_mine, g_other)


def gram(core, part, carried):
    channels, rows = carried.shape
    lower = lower_rows(channels)
    half = jax.ShapeDtypeStruct((lower // 2, LANES), jnp.float32)
    return pl.pallas_call(
        gram_kernel,
        in_specs=[SCALARS] + [WHOLE] * 2,
        out_specs=[WHOLE] * 3,
        out_shape=[jax.ShapeDtypeStruct((channels, rows), carried.dtype), half, half],
        scratch_shapes=[
            pltpu.VMEM((round_up(channels, LANES), rows), carried.dtype),
            pltpu.VMEM((lower, LANES), jnp.float32),
        ],
        compiler_params=params(),
        cost_estimate=cost(2 * channels * channels * rows, 8 * channels * rows),
    )(core, part, carried)


def split2(value):
    high = value.astype(jnp.bfloat16)
    return high, (value - high.astype(jnp.float32)).astype(jnp.bfloat16)


def store_payload(ref, mixed, ray):
    half = mixed.shape[0]
    high, low = split2(mixed)
    ref[0:half, :] = high
    ref[half : 2 * half, :] = low
    ref[2 * half : 3 * half, :] = ray.astype(jnp.bfloat16)


def load_payload(ref):
    half = ref.shape[0] // 3
    mixed = ref[0:half, :].astype(jnp.float32) + ref[half : 2 * half, :].astype(jnp.float32)
    return mixed, ref[2 * half : 3 * half, :].astype(jnp.float32)


def payload_shape(channels):
    return jax.ShapeDtypeStruct((3 * full_rows(channels) // 2, LANES), jnp.bfloat16)


def cross_kernel(
    core_ref, before_ref, x_ref, y_ref, after_ref, mine_ref, other_ref,
    left_ref, pad_ref, mixed_ref, ray_ref,
):
    channels = x_ref.shape[0]
    core = core_ref[0]
    half = mixed_ref.shape[0] // 2
    store_padded(pad_ref, y_ref[...])
    store_padded(left_ref, before_ref[...])
    full_products(left_ref, pad_ref, channels, mixed_ref)
    store_padded(left_ref, x_ref[...])
    full_products(left_ref, pad_ref, channels, ray_ref)
    mine = pl.ds(pl.multiple_of(core * half, 8), half)
    other = pl.ds(pl.multiple_of((1 - core) * half, 8), half)
    store_payload(mine_ref, mixed_ref[mine, :], ray_ref[mine, :])
    store_payload(other_ref, mixed_ref[other, :], ray_ref[other, :])


def cross(core, before, x_t, y_t, after):
    channels, rows = x_t.shape
    padded = pltpu.VMEM((round_up(channels, LANES), rows), x_t.dtype)
    pack = pltpu.VMEM((full_rows(channels), LANES), jnp.float32)
    return pl.pallas_call(
        cross_kernel,
        in_specs=[SCALARS, WHOLE, WHOLE, WHOLE, ANYWHERE],
        out_specs=[WHOLE] * 2,
        out_shape=[payload_shape(channels)] * 2,
        scratch_shapes=[padded, padded, pack, pack],
        compiler_params=params(),
        cost_estimate=cost(4 * channels * channels * rows, 6 * channels * rows),
    )(core, before, x_t, y_t, after)


def add_kernel(left_ref, right_ref, *refs):
    left, right = load_payload(left_ref), load_payload(right_ref)
    store_payload(refs[-1], left[0] + right[0], left[1] + right[1])


def last_add_kernel(left_ref, right_ref, mixed_ref, ray_ref):
    left, right = load_payload(left_ref), load_payload(right_ref)
    mixed_ref[...] = left[0] + right[0]
    ray_ref[...] = (left[1] + right[1]).astype(ray_ref.dtype)


def last_add(left, right):
    half = left.shape[0] // 3
    return pl.pallas_call(
        last_add_kernel,
        in_specs=[WHOLE] * 2,
        out_specs=[WHOLE] * 2,
        out_shape=[
            jax.ShapeDtypeStruct((half, LANES), jnp.float32),
            jax.ShapeDtypeStruct((half, LANES), jnp.bfloat16),
        ],
        compiler_params=params(),
        cost_estimate=cost(10**5, 10**5),
    )(left, right)


def add_payloads(left, right, *after):
    return pl.pallas_call(
        add_kernel,
        in_specs=[WHOLE] * 2 + [ANYWHERE] * len(after),
        out_specs=WHOLE,
        out_shape=jax.ShapeDtypeStruct(left.shape, left.dtype),
        compiler_params=params(),
        cost_estimate=cost(10**5, 10**6),
    )(left, right, *after)


def split3(value):
    high = value.astype(jnp.bfloat16)
    rest = value - high.astype(jnp.float32)
    mid = rest.astype(jnp.bfloat16)
    low = (rest - mid.astype(jnp.float32)).astype(jnp.bfloat16)
    return high, mid, low


def sublane(value, index):
    return jnp.broadcast_to(value[index : index + 1, :], value.shape)


def lane_of(value, index):
    return jnp.take_along_axis(value, jnp.broadcast_to(index, value.shape), axis=1)


def eliminate(columns, panel):
    half = 8
    row = lax.broadcasted_iota(jnp.int32, (half, LANES), 0)
    scales = [jnp.zeros((half, LANES), jnp.float32) for _ in range(2)]
    columns = [list(c) for c in columns]
    panel = [list(p) for p in panel]
    for j in range(PANEL):
        h, r = divmod(j, half)
        pivot = sublane(columns[j][h], r)
        inverse = lax.rsqrt(pivot)
        inverse = inverse * (1.5 - 0.5 * pivot * inverse * inverse)
        square = inverse * inverse
        factor = [None, None]
        factor[h] = jnp.where(row > r, columns[j][h], 0.0) * square
        if h == 0:
            factor[1] = columns[j][1] * square
        for later in range(j + 1, PANEL):
            entry = sublane(columns[j][later // half], later % half)
            for t in range(max(h, later // half), 2):
                columns[later][t] = columns[later][t] - factor[t] * entry
        for group in panel:
            entry = sublane(group[h], r)
            for t in range(h, 2):
                group[t] = group[t] - factor[t] * entry
        scales[h] = jnp.where(row == r, inverse, scales[h])
    return [jnp.concatenate([g[0] * scales[0], g[1] * scales[1]], axis=0) for g in panel]


def fill_work(channels, scale, pack_ref, work_ref):
    rows, wide = work_ref.shape
    groups = wide // LANES
    offset = 0
    for g in range(groups):
        top = g * LANES
        size = min(LANES, rows - top)
        column = pack_ref[offset : offset + rows - top, :] * scale
        offset += rows - top
        diag = column[0:size, :]
        if top + LANES > channels:
            row = lax.broadcasted_iota(jnp.int32, diag.shape, 0)
            lane = lax.broadcasted_iota(jnp.int32, diag.shape, 1)
            diag = jnp.where((row == lane) & (lane + top >= channels), 1.0, diag)
        work_ref[top : top + size, top : top + LANES] = diag
        for below in range(g + 1, groups):
            start = (below - g) * LANES
            size_b = min(LANES, rows - below * LANES)
            block = column[start : start + size_b, :]
            if size_b < LANES:
                block = jnp.concatenate(
                    [block, jnp.zeros((LANES - size_b, LANES), jnp.float32)], axis=0
                )
            work_ref[top : top + size, below * LANES : (below + 1) * LANES] = block.T
            work_ref[below * LANES : below * LANES + size_b, top : top + LANES] = jnp.zeros(
                (size_b, LANES), jnp.float32
            )


def eliminate_group(g, work_ref):
    rows, wide = work_ref.shape
    groups = wide // LANES
    row = lax.broadcasted_iota(jnp.int32, (PANEL, LANES), 0)
    lane = lax.broadcasted_iota(jnp.int32, (PANEL, LANES), 1)
    top = g * LANES
    size = min(LANES, rows - top)

    def step(b, carry):
        local = b * PANEL
        start = pl.multiple_of(top + local, PANEL)
        parts = [work_ref[pl.ds(start, PANEL), q * LANES : (q + 1) * LANES] for q in range(groups)]
        pivots = [parts[g][0:8, :], parts[g][8:16, :]]
        columns = [[lane_of(p, local + j) for p in pivots] for j in range(PANEL)]
        inside = (lane >= local) & (lane < local + PANEL)
        identity = jnp.where(lane - local == row, 1.0, 0.0)
        parts[g] = jnp.where(inside, identity, parts[g])
        done = eliminate(columns, [[p[0:8, :], p[8:16, :]] for p in parts])
        left, right = [], []
        for q in range(groups):
            high, mid, low = split3(done[q])
            right.append(jnp.concatenate([high, mid, high, low, mid, high], axis=0))
            if q >= g:
                if q == g:
                    high, mid, low = split3(jnp.where(lane >= local + PANEL, done[q], 0.0))
                left.append(jnp.concatenate([high, high, mid, high, mid, low], axis=0))
        for n, q in enumerate(range(g, groups)):
            low_row = q * LANES
            high_row = min(rows, low_row + LANES)
            for c in range(groups):
                update = dot(left[n], right[c], ((0,), (0,)))[0 : high_row - low_row, :]
                old = work_ref[low_row:high_row, c * LANES : (c + 1) * LANES]
                if c == g:
                    lanes = lax.broadcasted_iota(jnp.int32, old.shape, 1)
                    old = jnp.where((lanes >= local) & (lanes < local + PANEL), 0.0, old)
                work_ref[low_row:high_row, c * LANES : (c + 1) * LANES] = old - update
        for q in range(groups):
            if q == g:
                done[q] = jnp.where(lane < local + PANEL, done[q], 0.0)
            elif q > g:
                done[q] = jnp.zeros_like(done[q])
            work_ref[pl.ds(start, PANEL), q * LANES : (q + 1) * LANES] = done[q]
        return carry

    lax.fori_loop(0, size // PANEL, step, 0)


def first_stage_kernel(channels, scale, core_ref, mine_ref, other_ref, work_ref, pack_ref):
    join(pack_ref, core_ref[0], mine_ref[...], other_ref[...])
    fill_work(channels, scale, pack_ref, work_ref)
    eliminate_group(0, work_ref)


def last_stages_kernel(before_ref, after_ref, work_ref, pack_ref):
    work_ref[...] = before_ref[...]
    rows, wide = work_ref.shape
    for g in range(1, wide // LANES):
        eliminate_group(g, work_ref)
    offset = 0
    for q in range(wide // LANES):
        tall = rows - q * LANES
        pack_ref[offset : offset + tall, :] = work_ref[q * LANES : rows, q * LANES : (q + 1) * LANES]
        offset += tall


def work_shape(channels):
    return jax.ShapeDtypeStruct((round_up(channels, PANEL), round_up(channels, LANES)), jnp.float32)


def first_stage(core, mine, other, channels, total_rows):
    return pl.pallas_call(
        functools.partial(first_stage_kernel, channels, 1.0 / total_rows),
        in_specs=[SCALARS] + [WHOLE] * 2,
        out_specs=WHOLE,
        out_shape=work_shape(channels),
        scratch_shapes=[pltpu.VMEM((lower_rows(channels), LANES), jnp.float32)],
        compiler_params=params(),
        cost_estimate=cost(FIRST_STAGE_FLOPS, 10**6),
    )(core, mine, other)


def last_stages(work, channels, after):
    return pl.pallas_call(
        last_stages_kernel,
        in_specs=[WHOLE, ANYWHERE],
        out_specs=[WHOLE] * 2,
        out_shape=[
            work_shape(channels),
            jax.ShapeDtypeStruct((lower_rows(channels), LANES), jnp.float32),
        ],
        compiler_params=params(),
        cost_estimate=cost(LAST_STAGES_FLOPS, 10**5),
    )(work, after)


def dot3(left, right, dims):
    left_high, left_low = split2(left)
    right_high, right_low = split2(right)
    return (
        dot(left_high, right_high, dims)
        + dot(left_high, right_low, dims)
        + dot(left_low, right_high, dims)
    )


def lower_matrix(pack_ref, out_ref):
    rows, wide = out_ref.shape
    offset = 0
    for g in range(wide // LANES):
        top = g * LANES
        lanes = slice(top, top + LANES)
        if top:
            out_ref[0:top, lanes] = jnp.zeros((top, LANES), jnp.float32)
        out_ref[top:rows, lanes] = pack_ref[offset : offset + rows - top, :]
        offset += rows - top


def basis_kernel(inverse_ref, y_ref, q_ref):
    channels = y_ref.shape[0]
    image = y_ref[...]
    for start, size in strips(channels, 2 * LANES):
        used = min(channels, start + size)
        high, low = split2(inverse_ref[start : start + size, 0:used])
        both = dot(jnp.concatenate([high, low], axis=0), image[0:used, :], ((1,), (0,)))
        q_ref[start : start + size, :] = (both[0:size, :] + both[size:, :]).astype(q_ref.dtype)


def basis(inverse, y_t):
    channels, rows = y_t.shape
    return pl.pallas_call(
        basis_kernel,
        in_specs=[WHOLE] * 2,
        out_specs=WHOLE,
        out_shape=jax.ShapeDtypeStruct(y_t.shape, y_t.dtype),
        compiler_params=params(),
        cost_estimate=cost(10**5, 10**5),
    )(inverse, y_t)


def matrix_shape(channels):
    return jax.ShapeDtypeStruct((channels, 1, channels), jnp.float32)


def ray_kernel(scale, core_ref, mine_ref, other_ref, out_ref, pack_ref):
    channels = out_ref.shape[0]
    join(pack_ref, core_ref[0], mine_ref[...].astype(jnp.float32), other_ref[...].astype(jnp.float32))
    out_ref[:, 0, :] = full_matrix(pack_ref, channels)[0:channels, 0:channels] * scale


def unpack_ray(core, mine, other, channels, total_rows):
    return pl.pallas_call(
        functools.partial(ray_kernel, 1.0 / total_rows),
        in_specs=[SCALARS] + [WHOLE] * 2,
        out_specs=WHOLE,
        out_shape=matrix_shape(channels),
        scratch_shapes=[pltpu.VMEM((full_rows(channels), LANES), jnp.float32)],
        compiler_params=params(),
        cost_estimate=cost(10**5, 10**5),
    )(core, mine, other)


def half_kernel(core_ref, mine_ref, other_ref, inverse_ref, out_ref, pack_ref):
    join(pack_ref, core_ref[0], mine_ref[...], other_ref[...])
    mixed = full_matrix(pack_ref, inverse_ref.shape[0])
    out_ref[...] = dot3(mixed, inverse_ref[...], ((1,), (1,)))


def half_product(core, mine, other, inverse):
    rows = inverse.shape[0]
    return pl.pallas_call(
        half_kernel,
        in_specs=[SCALARS] + [WHOLE] * 3,
        out_specs=WHOLE,
        out_shape=jax.ShapeDtypeStruct((rows, rows), jnp.float32),
        scratch_shapes=[pltpu.VMEM((2 * mine.shape[0], LANES), jnp.float32)],
        compiler_params=params(),
        cost_estimate=cost(10**5, 10**5),
    )(core, mine, other, inverse)


def correlation_kernel(scale, previous_ref, half_ref, out_ref, before_ref):
    channels = out_ref.shape[0]
    rows = half_ref.shape[0]
    lower_matrix(previous_ref, before_ref)
    total = dot3(before_ref[:, 0:rows], half_ref[...], ((1,), (0,))) * scale
    out_ref[:, 0, :] = total[0:channels, 0:channels]


def correlate(previous, half, channels, total_rows):
    return pl.pallas_call(
        functools.partial(correlation_kernel, 1.0 / total_rows),
        in_specs=[WHOLE] * 2,
        out_specs=WHOLE,
        out_shape=matrix_shape(channels),
        scratch_shapes=[
            pltpu.VMEM((half.shape[0], round_up(channels, LANES)), jnp.float32),
        ],
        compiler_params=params(),
        cost_estimate=cost(10**8, 10**6),
    )(previous, half)


def from_behind(value, axis, steps):
    count = lax.axis_size(axis)
    leading, last = (max(0, -steps), min(count, count - steps))
    return lax.ppermute(value, axis, [(source, source + steps) for source in range(leading, last)])


def other_core(value):
    return lax.ppermute(value, "rows", [(s, s ^ 1) for s in range(lax.axis_size("rows"))])


def chip_rounds():
    count = lax.axis_size("rows")
    bits = []
    while 2 << len(bits) < count:
        bits.append(2 << len(bits))
    return [
        [(s, s ^ (bits[n] if s % 2 == 0 else bits[-1 - n])) for s in range(count)]
        for n in range(len(bits))
    ]


def shards(x_block, h_diag, h_right, pattern):
    x_t = x_block[0].T
    channels, block_rows = x_t.shape
    masks = pattern[0].transpose(1, 0, 2)
    total_rows = lax.axis_size("rows") * block_rows
    core = (lax.axis_index("rows") % 2).astype(jnp.int32).reshape(1)
    later = from_behind(x_t, "rows", -1)
    carried = from_behind(tile_product(1, masks, x_t, h_right[0], x_t.dtype, 58), "rows", 1)
    first = tile_product(0, masks, x_t, h_diag[0], jnp.float32, 50)
    part = later_product(masks, later, h_right[0], first)
    y_t, g_mine, g_other = gram(core, part, carried)
    previous_y = from_behind(y_t, "sector", 1)
    g_sum = g_mine + other_core(g_other)
    for pairs in chip_rounds():
        g_sum = g_sum + lax.ppermute(g_sum, "rows", pairs)
    work = first_stage(core, g_sum, other_core(g_sum), channels, total_rows)
    m_mine, m_other = cross(core, previous_y, x_t, y_t, work)
    m_sum = add_payloads(m_mine, other_core(m_other))
    work, pack = last_stages(work, channels, m_sum)
    previous = from_behind(pack, "sector", 1)
    q_t = basis(work, y_t)
    rounds = chip_rounds()
    for pairs in rounds[:-1]:
        m_sum = add_payloads(m_sum, lax.ppermute(m_sum, "rows", pairs), work)
    m_half, r_half = last_add(m_sum, lax.ppermute(m_sum, "rows", rounds[-1]))
    half = half_product(core, m_half, other_core(m_half), work)
    correlation = correlate(previous, half, channels, total_rows)
    rayleigh = unpack_ray(core, r_half, other_core(r_half), channels, total_rows)
    return (q_t.T[None], rayleigh.transpose(1, 0, 2), correlation.transpose(1, 0, 2))


def solution(mesh):
    in_specs = (
        P("sector", "rows", None),
        P("sector", "rows", None),
        P("sector", "rows", None),
        P("sector", None, "rows", None),
    )
    out_specs = (P("sector", "rows", None), P("sector", None, None), P("sector", None, None))
    return jax.shard_map(shards, mesh=mesh, in_specs=in_specs, out_specs=out_specs, check_vma=False)
```

profile of v0, /device:TPU:0, one launch (start us, length us, event | category | flops | bytes accessed | tf_op | source)
XLA Modules:
  0.0 69.1 jit_solution(16676222702350421436)
XLA Ops:
  0.6 1.4 %collective-permute-start = (bf16[300,1280]{1,0:T(8,128)(2,1)}, bf16[300,1280]{1,0:T(8,128)(2,1)S(1)}, u32[]{:S(2)}, u32[]{:S(2)}) collective-permute-start(bf16[300,1280]{1,0:T(8,128)(2,1)} %bitcast.14), channel_id=1, source_target_pairs={{1,0},{2,1},{3,2},{4,3},{5,4},{6,5},{7,6},{9,8},{10,9},{11,10},{12... | collective-permute-start | bytes 2304008 | tf_op jit(solution)/shard_map/ppermute | solution.py:632
  2.1 4.7 %shard_map.69 = bf16[300,1280]{1,0:T(8,128)(2,1)} custom-call(s32[10,2,10]{2,1,0:T(2,128)} %bitcast.18, bf16[300,1280]{1,0:T(8,128)(2,1)} %bitcast.15, bf16[1280,1280]{1,0:T(8,128)(2,1)} %bitcast.21), custom_call_target="tpu_custom_call" | custom-call | flops 983040000 | bytes 3276800 | tf_op jit(solution)/shard_map/pallas_call | solution.py:106
  6.8 3.1 %collective-permute-start.1 = (bf16[300,1280]{1,0:T(8,128)(2,1)}, bf16[300,1280]{1,0:T(8,128)(2,1)S(1)}, u32[]{:S(2)}, u32[]{:S(2)}) collective-permute-start(bf16[300,1280]{1,0:T(8,128)(2,1)} %shard_map.69), channel_id=1, source_target_pairs={{0,1},{1,2},{2,3},{3,4},{4,5},{5,6},{6,7},{8,9},{9,10},{10,11},{11... | collective-permute-start | bytes 2304008 | tf_op jit(solution)/shard_map/ppermute | solution.py:632
  9.9 3.3 %shard_map.67.first_ref = f32[300,1280]{1,0:T(8,128)S(1)} custom-call(s32[10,2,10]{2,1,0:T(2,128)S(1)} %bitcast.19, bf16[300,1280]{1,0:T(8,128)(2,1)S(1)} %bitcast.16, bf16[1280,1280]{1,0:T(8,128)(2,1)} %bitcast.23), custom_call_target="tpu_custom_call" | custom-call | flops 983040000 | bytes 3276800 | tf_op jit(solution)/shard_map/pallas_call | solution.py:106
  13.2 3.1 %shard_map.68.part_ref = f32[300,1280]{1,0:T(8,128)S(1)} custom-call(s32[10,2,10]{2,1,0:T(2,128)S(1)} %bitcast.20, bf16[300,1280]{1,0:T(8,128)(2,1)S(1)} %collective-permute-done.later_ref, bf16[1280,1280]{1,0:T(8,128)(2,1)} %bitcast.22, f32[300,1280]{1,0:T(8,128)S(1)} %shard_map.67.first_ref), custom_call_target="tpu_custom_call" | custom-call | flops 983040000 | bytes 3276800 | tf_op jit(solution)/shard_map/pallas_call | solution.py:141
  16.9 5.0 %collective-permute-start.6 = (bf16[300,1280]{1,0:T(8,128)(2,1)S(1)}, bf16[300,1280]{1,0:T(8,128)(2,1)S(1)}, u32[]{:S(2)}, u32[]{:S(2)}) collective-permute-start(bf16[300,1280]{1,0:T(8,128)(2,1)S(1)} %get-tuple-element.14.y_ref), channel_id=1, source_target_pairs={{0,8},{8,16},{16,24},{1,9},{9,17},{17,25},{2,10},{10,18},{18,26},{... | collective-permute-start | bytes 2304008 | tf_op jit(solution)/shard_map/ppermute | solution.py:632
  21.9 3.5 %collective-permute-start.2 = (f32[264,128]{1,0:T(8,128)S(1)}, f32[264,128]{1,0:T(8,128)S(1)}, u32[]{:S(2)}, u32[]{:S(2)}) collective-permute-start(f32[264,128]{1,0:T(8,128)S(1)} %get-tuple-element.13), channel_id=1, source_target_pairs={{0,1},{1,0},{2,3},{3,2},{4,5},{5,4},{6,7},{7,6},{8,9},{9,8},{10,11... | collective-permute-start | bytes 405512 | tf_op jit(solution)/shard_map/ppermute | solution.py:636
  25.5 1.0 %collective-permute-done.2 = f32[264,128]{1,0:T(8,128)S(1)} collective-permute-done((f32[264,128]{1,0:T(8,128)S(1)}, f32[264,128]{1,0:T(8,128)S(1)}, u32[]{:S(2)}, u32[]{:S(2)}) %collective-permute-start.2) | collective-permute-done | bytes 135200 | tf_op jit(solution)/shard_map/ppermute | solution.py:636
  26.5 3.0 %collective-permute-start.3 = (f32[264,128]{1,0:T(8,128)S(1)}, f32[264,128]{1,0:T(8,128)S(1)}, u32[]{:S(2)}, u32[]{:S(2)}) collective-permute-start(f32[264,128]{1,0:T(8,128)S(1)} %add.14), channel_id=1, source_target_pairs={{0,2},{1,5},{2,0},{3,7},{4,6},{5,1},{6,4},{7,3},{8,10},{9,13},{10,... | collective-permute-start | bytes 405512 | tf_op jit(solution)/shard_map/ppermute | solution.py:664
  29.4 3.0 %collective-permute-done.3 = f32[264,128]{1,0:T(8,128)S(1)} collective-permute-done((f32[264,128]{1,0:T(8,128)S(1)}, f32[264,128]{1,0:T(8,128)S(1)}, u32[]{:S(2)}, u32[]{:S(2)}) %collective-permute-start.3) | collective-permute-done | bytes 135200 | tf_op jit(solution)/shard_map/ppermute | solution.py:664
  32.5 3.9 %collective-permute-start.4 = (f32[264,128]{1,0:T(8,128)S(1)}, f32[264,128]{1,0:T(8,128)S(1)}, u32[]{:S(2)}, u32[]{:S(2)}) collective-permute-start(f32[264,128]{1,0:T(8,128)S(1)} %add.15), channel_id=1, source_target_pairs={{0,4},{1,3},{2,6},{3,1},{4,0},{5,7},{6,2},{7,5},{8,12},{9,11},{10,... | collective-permute-start | bytes 405512 | tf_op jit(solution)/shard_map/ppermute | solution.py:664
  36.3 3.0 %collective-permute-done.4 = f32[264,128]{1,0:T(8,128)S(1)} collective-permute-done((f32[264,128]{1,0:T(8,128)S(1)}, f32[264,128]{1,0:T(8,128)S(1)}, u32[]{:S(2)}, u32[]{:S(2)}) %collective-permute-start.4) | collective-permute-done | bytes 135200 | tf_op jit(solution)/shard_map/ppermute | solution.py:664
  39.4 1.3 %collective-permute-done.5.other_ref = f32[264,128]{1,0:T(8,128)S(1)} collective-permute-done((f32[264,128]{1,0:T(8,128)S(1)}, f32[264,128]{1,0:T(8,128)S(1)}, u32[]{:S(2)}, u32[]{:S(2)}) %collective-permute-start.5) | collective-permute-done | bytes 135200 | tf_op jit(solution)/shard_map/ppermute | solution.py:636
  40.8 4.9 %shard_map.71.after_ref.before_ref = f32[304,384]{1,0:T(8,128)S(1)} custom-call(s32[1]{0:T(128)} %bitcast.core_ref, f32[264,128]{1,0:T(8,128)S(1)} %add.16.mine_ref, f32[264,128]{1,0:T(8,128)S(1)} %collective-permute-done.5.other_ref), custom_call_target="tpu_custom_call" | custom-call | flops 2000000000 | bytes 1000000 | tf_op jit(solution)/shard_map/pallas_call | solution.py:497
  45.7 1.6 %shard_map.72 = (bf16[1152,128]{1,0:T(8,128)(2,1)S(1)}, bf16[1152,128]{1,0:T(8,128)(2,1)S(1)}) custom-call(s32[1]{0:T(128)} %bitcast.core_ref, bf16[300,1280]{1,0:T(8,128)(2,1)S(1)} %collective-permute-done.6.before_ref, bf16[300,1280]{1,0:T(8,128)(2,1)S(1)} %bitcast.17, bf16[300,1280]{1,0:T(8,128)(2,1)S(1)} %get-tuple-element.14.y_ref, ...), custom_call_target="tpu_custom_call" | custom-call | flops 460800000 | bytes 2304000 | tf_op jit(solution)/shard_map/pallas_call | solution.py:306
  47.5 1.4 %collective-permute-done.7.right_ref = bf16[1152,128]{1,0:T(8,128)(2,1)S(1)} collective-permute-done((bf16[1152,128]{1,0:T(8,128)(2,1)S(1)}, bf16[1152,128]{1,0:T(8,128)(2,1)S(1)}, u32[]{:S(2)}, u32[]{:S(2)}) %collective-permute-start.7) | collective-permute-done | bytes 294944 | tf_op jit(solution)/shard_map/ppermute | solution.py:636
  49.0 1.5 %collective-permute-start.8 = (bf16[1152,128]{1,0:T(8,128)(2,1)S(1)}, bf16[1152,128]{1,0:T(8,128)(2,1)S(1)}, u32[]{:S(2)}, u32[]{:S(2)}) collective-permute-start(bf16[1152,128]{1,0:T(8,128)(2,1)S(1)} %shard_map.73.after_ref.left_ref), channel_id=1, source_target_pairs={{0,2},{1,5},{2,0},{3,7},{4,6},{5,1},{6,4},{7,3},{8,10},{9,13},{10,... | collective-permute-start | bytes 884744 | tf_op jit(solution)/shard_map/ppermute | solution.py:673
  50.5 6.1 %shard_map.74 = (f32[304,384]{1,0:T(8,128)S(1)}, f32[528,128]{1,0:T(8,128)S(1)}) custom-call(f32[304,384]{1,0:T(8,128)S(1)} %shard_map.71.after_ref.before_ref, bf16[1152,128]{1,0:T(8,128)(2,1)S(1)} %shard_map.73.after_ref.left_ref), custom_call_target="tpu_custom_call" | custom-call | flops 4000000000 | bytes 100000 | tf_op jit(solution)/shard_map/pallas_call | solution.py:509
  56.6 2.1 %collective-permute-start.9 = (bf16[1152,128]{1,0:T(8,128)(2,1)S(1)}, bf16[1152,128]{1,0:T(8,128)(2,1)S(1)}, u32[]{:S(2)}, u32[]{:S(2)}) collective-permute-start(bf16[1152,128]{1,0:T(8,128)(2,1)S(1)} %shard_map.76.left_ref), channel_id=1, source_target_pairs={{0,4},{1,3},{2,6},{3,1},{4,0},{5,7},{6,2},{7,5},{8,12},{9,11},{10,... | collective-permute-start | bytes 884744 | tf_op jit(solution)/shard_map/ppermute | solution.py:674
  58.7 3.4 %collective-permute-start.11 = (f32[528,128]{1,0:T(8,128)S(1)}, f32[528,128]{1,0:T(8,128)S(1)}, u32[]{:S(2)}, u32[]{:S(2)}) collective-permute-start(f32[528,128]{1,0:T(8,128)S(1)} %get-tuple-element.19), channel_id=1, source_target_pairs={{0,8},{8,16},{16,24},{1,9},{9,17},{17,25},{2,10},{10,18},{18,26},{... | collective-permute-start | bytes 811016 | tf_op jit(solution)/shard_map/ppermute | solution.py:632
  62.2 1.3 %collective-permute-done.9.right_ref = bf16[1152,128]{1,0:T(8,128)(2,1)S(1)} collective-permute-done((bf16[1152,128]{1,0:T(8,128)(2,1)S(1)}, bf16[1152,128]{1,0:T(8,128)(2,1)S(1)}, u32[]{:S(2)}, u32[]{:S(2)}) %collective-permute-start.9) | collective-permute-done | bytes 294944 | tf_op jit(solution)/shard_map/ppermute | solution.py:674
  64.1 1.5 %shard_map.75 = bf16[300,1280]{1,0:T(8,128)(2,1)} custom-call(f32[304,384]{1,0:T(8,128)S(1)} %get-tuple-element.17.inverse_ref.refs_0_, bf16[300,1280]{1,0:T(8,128)(2,1)S(1)} %get-tuple-element.14.y_ref), custom_call_target="tpu_custom_call" | custom-call | flops 100000 | bytes 100000 | tf_op jit(solution)/shard_map/pallas_call | solution.py:556
  65.6 1.0 %shard_map.78 = f32[300,1,300]{2,1,0:T(1,128)} custom-call(s32[1]{0:T(128)} %bitcast.core_ref, bf16[384,128]{1,0:T(8,128)(2,1)S(1)} %get-tuple-element.18.mine_ref, bf16[384,128]{1,0:T(8,128)(2,1)S(1)} %collective-permute-done.10.other_ref), custom_call_target="tpu_custom_call" | custom-call | flops 100000 | bytes 100000 | tf_op jit(solution)/shard_map/pallas_call | solution.py:577
  67.6 1.5 %shard_map.80 = f32[300,1,300]{2,1,0:T(1,128)} custom-call(f32[528,128]{1,0:T(8,128)S(1)} %collective-permute-done.11.previous_ref, f32[304,304]{1,0:T(8,128)S(1)} %shard_map.79.half_ref), custom_call_target="tpu_custom_call" | custom-call | flops 100000000 | bytes 1000000 | tf_op jit(solution)/shard_map/pallas_call | solution.py:616
  (23 shorter events, 2.8 us)
Async XLA Ops:
  0.6 9.3 %copy-start = (bf16[1,1280,300]{1,2,0:T(8,128)(2,1)S(1)}, bf16[1,1280,300]{1,2,0:T(8,128)(2,1)}, u32[]{:S(2)}) copy-start(bf16[1,1280,300]{1,2,0:T(8,128)(2,1)} %param.4) | copy-start | bytes 2304004
  0.6 9.3 %copy-start.1 = (s32[1,2,10,10]{3,1,2,0:T(2,128)S(1)}, s32[1,2,10,10]{3,1,2,0:T(2,128)}, u32[]{:S(2)}) copy-start(s32[1,2,10,10]{3,1,2,0:T(2,128)} %param.7) | copy-start | bytes 2404
  0.6 12.5 %collective-permute-start = (bf16[300,1280]{1,0:T(8,128)(2,1)}, bf16[300,1280]{1,0:T(8,128)(2,1)S(1)}, u32[]{:S(2)}, u32[]{:S(2)}) collective-permute-start(bf16[300,1280]{1,0:T(8,128)(2,1)} %bitcast.14), channel_id=1, source_target_pairs={{1,0},{2,1},{3,2},{4,3},{5,4},{6,5},{7,6},{9,8},{10,9},{11,10},{12... | collective-permute-start | bytes 2304008 | tf_op jit(solution)/shard_map/ppermute | solution.py:632
  6.8 9.5 %collective-permute-start.1 = (bf16[300,1280]{1,0:T(8,128)(2,1)}, bf16[300,1280]{1,0:T(8,128)(2,1)S(1)}, u32[]{:S(2)}, u32[]{:S(2)}) collective-permute-start(bf16[300,1280]{1,0:T(8,128)(2,1)} %shard_map.69), channel_id=1, source_target_pairs={{0,1},{1,2},{2,3},{3,4},{4,5},{5,6},{6,7},{8,9},{9,10},{10,11},{11... | collective-permute-start | bytes 2304008 | tf_op jit(solution)/shard_map/ppermute | solution.py:632
  16.9 28.7 %collective-permute-start.6 = (bf16[300,1280]{1,0:T(8,128)(2,1)S(1)}, bf16[300,1280]{1,0:T(8,128)(2,1)S(1)}, u32[]{:S(2)}, u32[]{:S(2)}) collective-permute-start(bf16[300,1280]{1,0:T(8,128)(2,1)S(1)} %get-tuple-element.14.y_ref), channel_id=1, source_target_pairs={{0,8},{8,16},{16,24},{1,9},{9,17},{17,25},{2,10},{10,18},{18,26},{... | collective-permute-start | bytes 2304008 | tf_op jit(solution)/shard_map/ppermute | solution.py:632
  21.9 4.5 %collective-permute-start.2 = (f32[264,128]{1,0:T(8,128)S(1)}, f32[264,128]{1,0:T(8,128)S(1)}, u32[]{:S(2)}, u32[]{:S(2)}) collective-permute-start(f32[264,128]{1,0:T(8,128)S(1)} %get-tuple-element.13), channel_id=1, source_target_pairs={{0,1},{1,0},{2,3},{3,2},{4,5},{5,4},{6,7},{7,6},{8,9},{9,8},{10,11... | collective-permute-start | bytes 405512 | tf_op jit(solution)/shard_map/ppermute | solution.py:636
  26.5 6.0 %collective-permute-start.3 = (f32[264,128]{1,0:T(8,128)S(1)}, f32[264,128]{1,0:T(8,128)S(1)}, u32[]{:S(2)}, u32[]{:S(2)}) collective-permute-start(f32[264,128]{1,0:T(8,128)S(1)} %add.14), channel_id=1, source_target_pairs={{0,2},{1,5},{2,0},{3,7},{4,6},{5,1},{6,4},{7,3},{8,10},{9,13},{10,... | collective-permute-start | bytes 405512 | tf_op jit(solution)/shard_map/ppermute | solution.py:664
  32.5 6.9 %collective-permute-start.4 = (f32[264,128]{1,0:T(8,128)S(1)}, f32[264,128]{1,0:T(8,128)S(1)}, u32[]{:S(2)}, u32[]{:S(2)}) collective-permute-start(f32[264,128]{1,0:T(8,128)S(1)} %add.15), channel_id=1, source_target_pairs={{0,4},{1,3},{2,6},{3,1},{4,0},{5,7},{6,2},{7,5},{8,12},{9,11},{10,... | collective-permute-start | bytes 405512 | tf_op jit(solution)/shard_map/ppermute | solution.py:664
  39.3 1.4 %collective-permute-start.5 = (f32[264,128]{1,0:T(8,128)S(1)}, f32[264,128]{1,0:T(8,128)S(1)}, u32[]{:S(2)}, u32[]{:S(2)}) collective-permute-start(f32[264,128]{1,0:T(8,128)S(1)} %add.16.mine_ref), channel_id=1, source_target_pairs={{0,1},{1,0},{2,3},{3,2},{4,5},{5,4},{6,7},{7,6},{8,9},{9,8},{10,11... | collective-permute-start | bytes 405512 | tf_op jit(solution)/shard_map/ppermute | solution.py:636
  47.3 1.6 %collective-permute-start.7 = (bf16[1152,128]{1,0:T(8,128)(2,1)S(1)}, bf16[1152,128]{1,0:T(8,128)(2,1)S(1)}, u32[]{:S(2)}, u32[]{:S(2)}) collective-permute-start(bf16[1152,128]{1,0:T(8,128)(2,1)S(1)} %get-tuple-element.16), channel_id=1, source_target_pairs={{0,1},{1,0},{2,3},{3,2},{4,5},{5,4},{6,7},{7,6},{8,9},{9,8},{10,11... | collective-permute-start | bytes 884744 | tf_op jit(solution)/shard_map/ppermute | solution.py:636
  49.0 7.5 %collective-permute-start.8 = (bf16[1152,128]{1,0:T(8,128)(2,1)S(1)}, bf16[1152,128]{1,0:T(8,128)(2,1)S(1)}, u32[]{:S(2)}, u32[]{:S(2)}) collective-permute-start(bf16[1152,128]{1,0:T(8,128)(2,1)S(1)} %shard_map.73.after_ref.left_ref), channel_id=1, source_target_pairs={{0,2},{1,5},{2,0},{3,7},{4,6},{5,1},{6,4},{7,3},{8,10},{9,13},{10,... | collective-permute-start | bytes 884744 | tf_op jit(solution)/shard_map/ppermute | solution.py:673
  56.6 6.8 %collective-permute-start.9 = (bf16[1152,128]{1,0:T(8,128)(2,1)S(1)}, bf16[1152,128]{1,0:T(8,128)(2,1)S(1)}, u32[]{:S(2)}, u32[]{:S(2)}) collective-permute-start(bf16[1152,128]{1,0:T(8,128)(2,1)S(1)} %shard_map.76.left_ref), channel_id=1, source_target_pairs={{0,4},{1,3},{2,6},{3,1},{4,0},{5,7},{6,2},{7,5},{8,12},{9,11},{10,... | collective-permute-start | bytes 884744 | tf_op jit(solution)/shard_map/ppermute | solution.py:674
  58.7 8.9 %collective-permute-start.11 = (f32[528,128]{1,0:T(8,128)S(1)}, f32[528,128]{1,0:T(8,128)S(1)}, u32[]{:S(2)}, u32[]{:S(2)}) collective-permute-start(f32[528,128]{1,0:T(8,128)S(1)} %get-tuple-element.19), channel_id=1, source_target_pairs={{0,8},{8,16},{16,24},{1,9},{9,17},{17,25},{2,10},{10,18},{18,26},{... | collective-permute-start | bytes 811016 | tf_op jit(solution)/shard_map/ppermute | solution.py:632
  63.5 3.1 %collective-permute-start.12 = (f32[384,128]{1,0:T(8,128)S(1)}, f32[384,128]{1,0:T(8,128)S(1)}, u32[]{:S(2)}, u32[]{:S(2)}) collective-permute-start(f32[384,128]{1,0:T(8,128)S(1)} %get-tuple-element.20.mine_ref), channel_id=1, source_target_pairs={{0,1},{1,0},{2,3},{3,2},{4,5},{5,4},{6,7},{7,6},{8,9},{9,8},{10,11... | collective-permute-start | bytes 589832 | tf_op jit(solution)/shard_map/ppermute | solution.py:636
  63.6 2.0 %collective-permute-start.10 = (bf16[384,128]{1,0:T(8,128)(2,1)S(1)}, bf16[384,128]{1,0:T(8,128)(2,1)S(1)}, u32[]{:S(2)}, u32[]{:S(2)}) collective-permute-start(bf16[384,128]{1,0:T(8,128)(2,1)S(1)} %get-tuple-element.18.mine_ref), channel_id=1, source_target_pairs={{0,1},{1,0},{2,3},{3,2},{4,5},{5,4},{6,7},{7,6},{8,9},{9,8},{10,11... | collective-permute-start | bytes 294920 | tf_op jit(solution)/shard_map/ppermute | solution.py:636
where the time goes:
time: 69.4 us; the launch traced here: 69.1 us
  Pallas kernels  29.1 us (42%)
  starting transfers between devices  27.7 us (40%)
  waiting for transfers between devices  11.4 us (16%)
  between operations  0.84 us (1%)
    ppermute x4, starting transfers between devices, from_behind(): lax.ppermute(value, axis, [(source, source + steps) for source in range(l...  12.9 us
    pallas_call x2, Pallas kernels, tile_product(): pl.pallas_call(functools.partial(tile_kernel, which), in_specs=[WHOLE, AN...  7.97 us
    ppermute x2, starting transfers between devices, shards(): g_sum = g_sum + lax.ppermute(g_sum, 'rows', pairs)  6.84 us
    pallas_call x1, Pallas kernels, last_stages(): pl.pallas_call(last_stages_kernel, in_specs=[WHOLE, ANYWHERE], out_specs=...  6.07 us
    ppermute x2, waiting for transfers between devices, shards(): g_sum = g_sum + lax.ppermute(g_sum, 'rows', pairs)  5.98 us
    pallas_call x1, Pallas kernels, first_stage(): pl.pallas_call(functools.partial(first_stage_kernel, channels, 1.0 / tota...  4.88 us
    ppermute x5, starting transfers between devices, other_core(): lax.ppermute(value, 'rows', [(s, s ^ 1) for s in range(lax.axis_size('row...  4.41 us
    ppermute x5, waiting for transfers between devices, other_core(): lax.ppermute(value, 'rows', [(s, s ^ 1) for s in range(lax.axis_size('row...  3.76 us
  transfers between devices with their start and end apart: 13, of which 7 were waited for; matrix products, arithmetic and copies ran while one was open for 0% of the time, Pallas kernels for 37%

commit v1 on v0

--- a/solution.py
+++ b/solution.py
@@ -14,7 +14,7 @@
 SCALARS = pl.BlockSpec(memory_space=pltpu.SMEM)
 ANYWHERE = pl.BlockSpec(memory_space=pl.ANY)
 MIB = 1024 * 1024
-FIRST_STAGE_FLOPS = 2 * 10**9
+FIRST_STAGE_FLOPS = 3 * 10**9
 LAST_STAGES_FLOPS = 4 * 10**9
 
 
@@ -319,17 +319,17 @@
     store_payload(refs[-1], left[0] + right[0], left[1] + right[1])
 
 
-def last_add_kernel(left_ref, right_ref, mixed_ref, ray_ref):
+def last_add_kernel(left_ref, right_ref, after_ref, mixed_ref, ray_ref):
     left, right = load_payload(left_ref), load_payload(right_ref)
     mixed_ref[...] = left[0] + right[0]
     ray_ref[...] = (left[1] + right[1]).astype(ray_ref.dtype)
 
 
-def last_add(left, right):
+def last_add(left, right, after):
     half = left.shape[0] // 3
     return pl.pallas_call(
         last_add_kernel,
-        in_specs=[WHOLE] * 2,
+        in_specs=[WHOLE] * 2 + [ANYWHERE],
         out_specs=[WHOLE] * 2,
         out_shape=[
             jax.ShapeDtypeStruct((half, LANES), jnp.float32),
@@ -337,7 +337,7 @@
         ],
         compiler_params=params(),
         cost_estimate=cost(10**5, 10**5),
-    )(left, right)
+    )(left, right, after)
 
 
 def add_payloads(left, right, *after):
@@ -541,9 +541,10 @@
         offset += rows - top
 
 
-def basis_kernel(inverse_ref, y_ref, q_ref):
+def basis_kernel(inverse_ref, y_ref, q_ref, token_ref):
     channels = y_ref.shape[0]
     image = y_ref[...]
+    token_ref[...] = jnp.zeros_like(token_ref)
     for start, size in strips(channels, 2 * LANES):
         used = min(channels, start + size)
         high, low = split2(inverse_ref[start : start + size, 0:used])
@@ -556,8 +557,11 @@
     return pl.pallas_call(
         basis_kernel,
         in_specs=[WHOLE] * 2,
-        out_specs=WHOLE,
-        out_shape=jax.ShapeDtypeStruct(y_t.shape, y_t.dtype),
+        out_specs=[WHOLE] * 2,
+        out_shape=[
+            jax.ShapeDtypeStruct(y_t.shape, y_t.dtype),
+            jax.ShapeDtypeStruct((8, LANES), jnp.float32),
+        ],
         compiler_params=params(),
         cost_estimate=cost(10**5, 10**5),
     )(inverse, y_t)
@@ -654,7 +658,7 @@
     total_rows = lax.axis_size("rows") * block_rows
     core = (lax.axis_index("rows") % 2).astype(jnp.int32).reshape(1)
     later = from_behind(x_t, "rows", -1)
-    carried = from_behind(tile_product(1, masks, x_t, h_right[0], x_t.dtype, 58), "rows", 1)
+    carried = from_behind(tile_product(1, masks, x_t, h_right[0], x_t.dtype, 53), "rows", 1)
     first = tile_product(0, masks, x_t, h_diag[0], jnp.float32, 50)
     part = later_product(masks, later, h_right[0], first)
     y_t, g_mine, g_other = gram(core, part, carried)
@@ -667,11 +671,11 @@
     m_sum = add_payloads(m_mine, other_core(m_other))
     work, pack = last_stages(work, channels, m_sum)
     previous = from_behind(pack, "sector", 1)
-    q_t = basis(work, y_t)
+    q_t, token = basis(work, y_t)
     rounds = chip_rounds()
     for pairs in rounds[:-1]:
         m_sum = add_payloads(m_sum, lax.ppermute(m_sum, "rows", pairs), work)
-    m_half, r_half = last_add(m_sum, lax.ppermute(m_sum, "rows", rounds[-1]))
+    m_half, r_half = last_add(m_sum, lax.ppermute(m_sum, "rows", rounds[-1]), token)
     half = half_product(core, m_half, other_core(m_half), work)
     correlation = correlate(previous, half, channels, total_rows)
     rayleigh = unpack_ray(core, r_half, other_core(r_half), channels, total_rows)

time: 69.4 us -> 69.7 us (level)
  starting transfers between devices: 27.7 us -> 29.8 us
  Pallas kernels: 29.1 us -> 27.6 us
  waiting for transfers between devices: 11.4 us -> 10.4 us
    pallas_call x2, Pallas kernels: 7.97 us -> 6.41 us  [tile_product(): pl.pallas_call(functools.partial(tile_kernel, which), in_specs=[WHOLE, AN...]
    ppermute x5, starting transfers between devices: 4.41 us -> 5.76 us  [other_core(): lax.ppermute(value, 'rows', [(s, s ^ 1) for s in range(lax.axis_size('row...]
    ppermute x1, waiting for transfers between devices: 1.26 us -> 0.01 us  [shards(): lax.ppermute(m_sum, 'rows', rounds[-1])]
  transfers between devices with their start and end apart: 13 -> 13, of which waited for: 7 -> 6; matrix products, arithmetic and copies ran while one was open for 0% -> 0% of each run, Pallas kernels for 37% -> 34%
where the time goes in v1:
time: 69.7 us; the launch traced here: 69.4 us
  starting transfers between devices  29.8 us (43%)
  Pallas kernels  27.6 us (40%)
  waiting for transfers between devices  10.4 us (15%)
  between operations  0.85 us (1%)
  local copies, waits for them, and re-layouts  0.7 us (1%)
    ppermute x4, starting transfers between devices, from_behind(): lax.ppermute(value, axis, [(source, source + steps) for source in range(l...  12.4 us
    ppermute x2, starting transfers between devices, shards(): g_sum = g_sum + lax.ppermute(g_sum, 'rows', pairs)  7.33 us
    pallas_call x2, Pallas kernels, tile_product(): pl.pallas_call(functools.partial(tile_kernel, which), in_specs=[WHOLE, AN...  6.41 us
    pallas_call x1, Pallas kernels, last_stages(): pl.pallas_call(last_stages_kernel, in_specs=[WHOLE, ANYWHERE], out_specs=...  6.07 us
    ppermute x2, waiting for transfers between devices, shards(): g_sum = g_sum + lax.ppermute(g_sum, 'rows', pairs)  5.98 us
    ppermute x5, starting transfers between devices, other_core(): lax.ppermute(value, 'rows', [(s, s ^ 1) for s in range(lax.axis_size('row...  5.76 us
    pallas_call x1, Pallas kernels, first_stage(): pl.pallas_call(functools.partial(first_stage_kernel, channels, 1.0 / tota...  4.88 us
    ppermute x5, waiting for transfers between devices, other_core(): lax.ppermute(value, 'rows', [(s, s ^ 1) for s in range(lax.axis_size('row...  3.86 us
  transfers between devices with their start and end apart: 13, of which 6 were waited for; matrix products, arithmetic and copies ran while one was open for 0% of the time, Pallas kernels for 34%

profile of v1, /device:TPU:0, one launch (start us, length us, event | category | flops | bytes accessed | tf_op | source)
XLA Modules:
  0.0 69.4 jit_solution(9646011722325836836)
XLA Ops:
  0.6 1.4 %collective-permute-start = (bf16[300,1280]{1,0:T(8,128)(2,1)}, bf16[300,1280]{1,0:T(8,128)(2,1)S(1)}, u32[]{:S(2)}, u32[]{:S(2)}) collective-permute-start(bf16[300,1280]{1,0:T(8,128)(2,1)} %bitcast.14), channel_id=1, source_target_pairs={{1,0},{2,1},{3,2},{4,3},{5,4},{6,5},{7,6},{9,8},{10,9},{11,10},{12... | collective-permute-start | bytes 2304008 | tf_op jit(solution)/shard_map/ppermute | solution.py:636
  2.1 0.7 copy-done.1
  2.8 3.1 %shard_map.69 = bf16[300,1280]{1,0:T(8,128)(2,1)S(1)} custom-call(s32[10,2,10]{2,1,0:T(2,128)S(1)} %bitcast.18, bf16[300,1280]{1,0:T(8,128)(2,1)} %bitcast.15, bf16[1280,1280]{1,0:T(8,128)(2,1)} %bitcast.21), custom_call_target="tpu_custom_call" | custom-call | flops 983040000 | bytes 3276800 | tf_op jit(solution)/shard_map/pallas_call | solution.py:106
  5.9 3.1 %collective-permute-start.1 = (bf16[300,1280]{1,0:T(8,128)(2,1)S(1)}, bf16[300,1280]{1,0:T(8,128)(2,1)S(1)}, u32[]{:S(2)}, u32[]{:S(2)}) collective-permute-start(bf16[300,1280]{1,0:T(8,128)(2,1)S(1)} %shard_map.69), channel_id=1, source_target_pairs={{0,1},{1,2},{2,3},{3,4},{4,5},{5,6},{6,7},{8,9},{9,10},{10,11},{11... | collective-permute-start | bytes 2304008 | tf_op jit(solution)/shard_map/ppermute | solution.py:636
  9.0 3.3 %shard_map.67.first_ref = f32[300,1280]{1,0:T(8,128)S(1)} custom-call(s32[10,2,10]{2,1,0:T(2,128)S(1)} %bitcast.19, bf16[300,1280]{1,0:T(8,128)(2,1)S(1)} %bitcast.16, bf16[1280,1280]{1,0:T(8,128)(2,1)} %bitcast.23), custom_call_target="tpu_custom_call" | custom-call | flops 983040000 | bytes 3276800 | tf_op jit(solution)/shard_map/pallas_call | solution.py:106
  12.3 3.1 %shard_map.68.part_ref = f32[300,1280]{1,0:T(8,128)S(1)} custom-call(s32[10,2,10]{2,1,0:T(2,128)S(1)} %bitcast.20, bf16[300,1280]{1,0:T(8,128)(2,1)S(1)} %collective-permute-done.later_ref, bf16[1280,1280]{1,0:T(8,128)(2,1)} %bitcast.22, f32[300,1280]{1,0:T(8,128)S(1)} %shard_map.67.first_ref), custom_call_target="tpu_custom_call" | custom-call | flops 983040000 | bytes 3276800 | tf_op jit(solution)/shard_map/pallas_call | solution.py:141
  16.1 4.9 %collective-permute-start.2 = (f32[264,128]{1,0:T(8,128)S(1)}, f32[264,128]{1,0:T(8,128)S(1)}, u32[]{:S(2)}, u32[]{:S(2)}) collective-permute-start(f32[264,128]{1,0:T(8,128)S(1)} %get-tuple-element.15), channel_id=1, source_target_pairs={{0,1},{1,0},{2,3},{3,2},{4,5},{5,4},{6,7},{7,6},{8,9},{9,8},{10,11... | collective-permute-start | bytes 405512 | tf_op jit(solution)/shard_map/ppermute | solution.py:640
  21.0 3.5 %collective-permute-start.6 = (bf16[300,1280]{1,0:T(8,128)(2,1)S(1)}, bf16[300,1280]{1,0:T(8,128)(2,1)S(1)}, u32[]{:S(2)}, u32[]{:S(2)}) collective-permute-start(bf16[300,1280]{1,0:T(8,128)(2,1)S(1)} %get-tuple-element.16.y_ref), channel_id=1, source_target_pairs={{0,8},{8,16},{16,24},{1,9},{9,17},{17,25},{2,10},{10,18},{18,26},{... | collective-permute-start | bytes 2304008 | tf_op jit(solution)/shard_map/ppermute | solution.py:636
  24.6 3.4 %collective-permute-start.3 = (f32[264,128]{1,0:T(8,128)S(1)}, f32[264,128]{1,0:T(8,128)S(1)}, u32[]{:S(2)}, u32[]{:S(2)}) collective-permute-start(f32[264,128]{1,0:T(8,128)S(1)} %add.14), channel_id=1, source_target_pairs={{0,2},{1,5},{2,0},{3,7},{4,6},{5,1},{6,4},{7,3},{8,10},{9,13},{10,... | collective-permute-start | bytes 405512 | tf_op jit(solution)/shard_map/ppermute | solution.py:668
  28.0 3.0 %collective-permute-done.3 = f32[264,128]{1,0:T(8,128)S(1)} collective-permute-done((f32[264,128]{1,0:T(8,128)S(1)}, f32[264,128]{1,0:T(8,128)S(1)}, u32[]{:S(2)}, u32[]{:S(2)}) %collective-permute-start.3) | collective-permute-done | bytes 135200 | tf_op jit(solution)/shard_map/ppermute | solution.py:668
  31.0 3.9 %collective-permute-start.4 = (f32[264,128]{1,0:T(8,128)S(1)}, f32[264,128]{1,0:T(8,128)S(1)}, u32[]{:S(2)}, u32[]{:S(2)}) collective-permute-start(f32[264,128]{1,0:T(8,128)S(1)} %add.15), channel_id=1, source_target_pairs={{0,4},{1,3},{2,6},{3,1},{4,0},{5,7},{6,2},{7,5},{8,12},{9,11},{10,... | collective-permute-start | bytes 405512 | tf_op jit(solution)/shard_map/ppermute | solution.py:668
  34.9 3.0 %collective-permute-done.4 = f32[264,128]{1,0:T(8,128)S(1)} collective-permute-done((f32[264,128]{1,0:T(8,128)S(1)}, f32[264,128]{1,0:T(8,128)S(1)}, u32[]{:S(2)}, u32[]{:S(2)}) %collective-permute-start.4) | collective-permute-done | bytes 135200 | tf_op jit(solution)/shard_map/ppermute | solution.py:668
  38.0 1.3 %collective-permute-done.5.other_ref = f32[264,128]{1,0:T(8,128)S(1)} collective-permute-done((f32[264,128]{1,0:T(8,128)S(1)}, f32[264,128]{1,0:T(8,128)S(1)}, u32[]{:S(2)}, u32[]{:S(2)}) %collective-permute-start.5) | collective-permute-done | bytes 135200 | tf_op jit(solution)/shard_map/ppermute | solution.py:640
  39.4 4.9 %shard_map.71.after_ref.before_ref = f32[304,384]{1,0:T(8,128)S(1)} custom-call(s32[1]{0:T(128)} %bitcast.core_ref, f32[264,128]{1,0:T(8,128)S(1)} %add.16.mine_ref, f32[264,128]{1,0:T(8,128)S(1)} %collective-permute-done.5.other_ref), custom_call_target="tpu_custom_call" | custom-call | flops 3000000000 | bytes 1000000 | tf_op jit(solution)/shard_map/pallas_call | solution.py:497
  44.3 1.6 %shard_map.72 = (bf16[1152,128]{1,0:T(8,128)(2,1)S(1)}, bf16[1152,128]{1,0:T(8,128)(2,1)S(1)}) custom-call(s32[1]{0:T(128)} %bitcast.core_ref, bf16[300,1280]{1,0:T(8,128)(2,1)S(1)} %collective-permute-done.6.before_ref, bf16[300,1280]{1,0:T(8,128)(2,1)S(1)} %bitcast.17, bf16[300,1280]{1,0:T(8,128)(2,1)S(1)} %get-tuple-element.16.y_ref, ...), custom_call_target="tpu_custom_call" | custom-call | flops 460800000 | bytes 2304000 | tf_op jit(solution)/shard_map/pallas_call | solution.py:306
  46.1 1.4 %collective-permute-done.7.right_ref = bf16[1152,128]{1,0:T(8,128)(2,1)S(1)} collective-permute-done((bf16[1152,128]{1,0:T(8,128)(2,1)S(1)}, bf16[1152,128]{1,0:T(8,128)(2,1)S(1)}, u32[]{:S(2)}, u32[]{:S(2)}) %collective-permute-start.7) | collective-permute-done | bytes 294944 | tf_op jit(solution)/shard_map/ppermute | solution.py:640
  47.6 1.5 %collective-permute-start.8 = (bf16[1152,128]{1,0:T(8,128)(2,1)S(1)}, bf16[1152,128]{1,0:T(8,128)(2,1)S(1)}, u32[]{:S(2)}, u32[]{:S(2)}) collective-permute-start(bf16[1152,128]{1,0:T(8,128)(2,1)S(1)} %shard_map.73.after_ref.left_ref), channel_id=1, source_target_pairs={{0,2},{1,5},{2,0},{3,7},{4,6},{5,1},{6,4},{7,3},{8,10},{9,13},{10,... | collective-permute-start | bytes 884744 | tf_op jit(solution)/shard_map/ppermute | solution.py:677
  49.1 6.1 %shard_map.74 = (f32[304,384]{1,0:T(8,128)S(1)}, f32[528,128]{1,0:T(8,128)S(1)}) custom-call(f32[304,384]{1,0:T(8,128)S(1)} %shard_map.71.after_ref.before_ref, bf16[1152,128]{1,0:T(8,128)(2,1)S(1)} %shard_map.73.after_ref.left_ref), custom_call_target="tpu_custom_call" | custom-call | flops 4000000000 | bytes 100000 | tf_op jit(solution)/shard_map/pallas_call | solution.py:509
  55.3 2.7 %collective-permute-start.9 = (bf16[1152,128]{1,0:T(8,128)(2,1)S(1)}, bf16[1152,128]{1,0:T(8,128)(2,1)S(1)}, u32[]{:S(2)}, u32[]{:S(2)}) collective-permute-start(bf16[1152,128]{1,0:T(8,128)(2,1)S(1)} %shard_map.76.left_ref), channel_id=1, source_target_pairs={{0,4},{1,3},{2,6},{3,1},{4,0},{5,7},{6,2},{7,5},{8,12},{9,11},{10,... | collective-permute-start | bytes 884744 | tf_op jit(solution)/shard_map/ppermute | solution.py:678
  58.1 4.4 %collective-permute-start.11 = (f32[528,128]{1,0:T(8,128)S(1)}, f32[528,128]{1,0:T(8,128)S(1)}, u32[]{:S(2)}, u32[]{:S(2)}) collective-permute-start(f32[528,128]{1,0:T(8,128)S(1)} %get-tuple-element.23), channel_id=1, source_target_pairs={{0,8},{8,16},{16,24},{1,9},{9,17},{17,25},{2,10},{10,18},{18,26},{... | collective-permute-start | bytes 811016 | tf_op jit(solution)/shard_map/ppermute | solution.py:636
  62.5 1.5 %shard_map.75 = (bf16[300,1280]{1,0:T(8,128)(2,1)}, f32[8,128]{1,0:T(8,128)S(1)}) custom-call(f32[304,384]{1,0:T(8,128)S(1)} %get-tuple-element.19.inverse_ref.refs_0_, bf16[300,1280]{1,0:T(8,128)(2,1)S(1)} %get-tuple-element.16.y_ref), custom_call_target="tpu_custom_call" | custom-call | flops 100000 | bytes 100000 | tf_op jit(solution)/shard_map/pallas_call | solution.py:557
  64.7 1.1 %collective-permute-done.10.other_ref = bf16[384,128]{1,0:T(8,128)(2,1)S(1)} collective-permute-done((bf16[384,128]{1,0:T(8,128)(2,1)S(1)}, bf16[384,128]{1,0:T(8,128)(2,1)S(1)}, u32[]{:S(2)}, u32[]{:S(2)}) %collective-permute-start.10) | collective-permute-done | bytes 98336 | tf_op jit(solution)/shard_map/ppermute | solution.py:640
  65.7 1.0 %shard_map.78 = f32[300,1,300]{2,1,0:T(1,128)} custom-call(s32[1]{0:T(128)} %bitcast.core_ref, bf16[384,128]{1,0:T(8,128)(2,1)S(1)} %get-tuple-element.22.mine_ref, bf16[384,128]{1,0:T(8,128)(2,1)S(1)} %collective-permute-done.10.other_ref), custom_call_target="tpu_custom_call" | custom-call | flops 100000 | bytes 100000 | tf_op jit(solution)/shard_map/pallas_call | solution.py:581
  67.9 1.5 %shard_map.80 = f32[300,1,300]{2,1,0:T(1,128)} custom-call(f32[528,128]{1,0:T(8,128)S(1)} %collective-permute-done.11.previous_ref, f32[304,304]{1,0:T(8,128)S(1)} %shard_map.79.half_ref), custom_call_target="tpu_custom_call" | custom-call | flops 100000000 | bytes 1000000 | tf_op jit(solution)/shard_map/pallas_call | solution.py:620
  (25 shorter events, 3.0 us)
Async XLA Ops:
  0.6 8.4 %copy-start = (bf16[1,1280,300]{1,2,0:T(8,128)(2,1)S(1)}, bf16[1,1280,300]{1,2,0:T(8,128)(2,1)}, u32[]{:S(2)}) copy-start(bf16[1,1280,300]{1,2,0:T(8,128)(2,1)} %param.4) | copy-start | bytes 2304004
  0.6 11.7 %collective-permute-start = (bf16[300,1280]{1,0:T(8,128)(2,1)}, bf16[300,1280]{1,0:T(8,128)(2,1)S(1)}, u32[]{:S(2)}, u32[]{:S(2)}) collective-permute-start(bf16[300,1280]{1,0:T(8,128)(2,1)} %bitcast.14), channel_id=1, source_target_pairs={{1,0},{2,1},{3,2},{4,3},{5,4},{6,5},{7,6},{9,8},{10,9},{11,10},{12... | collective-permute-start | bytes 2304008 | tf_op jit(solution)/shard_map/ppermute | solution.py:636
  2.1 0.7 %copy-start.1 = (s32[1,2,10,10]{3,1,2,0:T(2,128)S(1)}, s32[1,2,10,10]{3,1,2,0:T(2,128)}, u32[]{:S(2)}) copy-start(s32[1,2,10,10]{3,1,2,0:T(2,128)} %param.7) | copy-start | bytes 2404
  2.8 6.3 %copy-start.2 = (s32[1,2,10,10]{3,1,2,0:T(2,128)S(1)}, s32[1,2,10,10]{3,1,2,0:T(2,128)}, u32[]{:S(2)}) copy-start(s32[1,2,10,10]{3,1,2,0:T(2,128)} %param.7) | copy-start | bytes 2404
  5.9 9.6 %collective-permute-start.1 = (bf16[300,1280]{1,0:T(8,128)(2,1)S(1)}, bf16[300,1280]{1,0:T(8,128)(2,1)S(1)}, u32[]{:S(2)}, u32[]{:S(2)}) collective-permute-start(bf16[300,1280]{1,0:T(8,128)(2,1)S(1)} %shard_map.69), channel_id=1, source_target_pairs={{0,1},{1,2},{2,3},{3,4},{4,5},{5,6},{6,7},{8,9},{9,10},{10,11},{11... | collective-permute-start | bytes 2304008 | tf_op jit(solution)/shard_map/ppermute | solution.py:636
  16.1 8.4 %collective-permute-start.2 = (f32[264,128]{1,0:T(8,128)S(1)}, f32[264,128]{1,0:T(8,128)S(1)}, u32[]{:S(2)}, u32[]{:S(2)}) collective-permute-start(f32[264,128]{1,0:T(8,128)S(1)} %get-tuple-element.15), channel_id=1, source_target_pairs={{0,1},{1,0},{2,3},{3,2},{4,5},{5,4},{6,7},{7,6},{8,9},{9,8},{10,11... | collective-permute-start | bytes 405512 | tf_op jit(solution)/shard_map/ppermute | solution.py:640
  21.0 23.2 %collective-permute-start.6 = (bf16[300,1280]{1,0:T(8,128)(2,1)S(1)}, bf16[300,1280]{1,0:T(8,128)(2,1)S(1)}, u32[]{:S(2)}, u32[]{:S(2)}) collective-permute-start(bf16[300,1280]{1,0:T(8,128)(2,1)S(1)} %get-tuple-element.16.y_ref), channel_id=1, source_target_pairs={{0,8},{8,16},{16,24},{1,9},{9,17},{17,25},{2,10},{10,18},{18,26},{... | collective-permute-start | bytes 2304008 | tf_op jit(solution)/shard_map/ppermute | solution.py:636
  24.6 6.4 %collective-permute-start.3 = (f32[264,128]{1,0:T(8,128)S(1)}, f32[264,128]{1,0:T(8,128)S(1)}, u32[]{:S(2)}, u32[]{:S(2)}) collective-permute-start(f32[264,128]{1,0:T(8,128)S(1)} %add.14), channel_id=1, source_target_pairs={{0,2},{1,5},{2,0},{3,7},{4,6},{5,1},{6,4},{7,3},{8,10},{9,13},{10,... | collective-permute-start | bytes 405512 | tf_op jit(solution)/shard_map/ppermute | solution.py:668
  31.0 6.9 %collective-permute-start.4 = (f32[264,128]{1,0:T(8,128)S(1)}, f32[264,128]{1,0:T(8,128)S(1)}, u32[]{:S(2)}, u32[]{:S(2)}) collective-permute-start(f32[264,128]{1,0:T(8,128)S(1)} %add.15), channel_id=1, source_target_pairs={{0,4},{1,3},{2,6},{3,1},{4,0},{5,7},{6,2},{7,5},{8,12},{9,11},{10,... | collective-permute-start | bytes 405512 | tf_op jit(solution)/shard_map/ppermute | solution.py:668
  38.0 1.4 %collective-permute-start.5 = (f32[264,128]{1,0:T(8,128)S(1)}, f32[264,128]{1,0:T(8,128)S(1)}, u32[]{:S(2)}, u32[]{:S(2)}) collective-permute-start(f32[264,128]{1,0:T(8,128)S(1)} %add.16.mine_ref), channel_id=1, source_target_pairs={{0,1},{1,0},{2,3},{3,2},{4,5},{5,4},{6,7},{7,6},{8,9},{9,8},{10,11... | collective-permute-start | bytes 405512 | tf_op jit(solution)/shard_map/ppermute | solution.py:640
  45.9 1.6 %collective-permute-start.7 = (bf16[1152,128]{1,0:T(8,128)(2,1)S(1)}, bf16[1152,128]{1,0:T(8,128)(2,1)S(1)}, u32[]{:S(2)}, u32[]{:S(2)}) collective-permute-start(bf16[1152,128]{1,0:T(8,128)(2,1)S(1)} %get-tuple-element.18), channel_id=1, source_target_pairs={{0,1},{1,0},{2,3},{3,2},{4,5},{5,4},{6,7},{7,6},{8,9},{9,8},{10,11... | collective-permute-start | bytes 884744 | tf_op jit(solution)/shard_map/ppermute | solution.py:640
  47.6 7.6 %collective-permute-start.8 = (bf16[1152,128]{1,0:T(8,128)(2,1)S(1)}, bf16[1152,128]{1,0:T(8,128)(2,1)S(1)}, u32[]{:S(2)}, u32[]{:S(2)}) collective-permute-start(bf16[1152,128]{1,0:T(8,128)(2,1)S(1)} %shard_map.73.after_ref.left_ref), channel_id=1, source_target_pairs={{0,2},{1,5},{2,0},{3,7},{4,6},{5,1},{6,4},{7,3},{8,10},{9,13},{10,... | collective-permute-start | bytes 884744 | tf_op jit(solution)/shard_map/ppermute | solution.py:677
  55.3 8.7 %collective-permute-start.9 = (bf16[1152,128]{1,0:T(8,128)(2,1)S(1)}, bf16[1152,128]{1,0:T(8,128)(2,1)S(1)}, u32[]{:S(2)}, u32[]{:S(2)}) collective-permute-start(bf16[1152,128]{1,0:T(8,128)(2,1)S(1)} %shard_map.76.left_ref), channel_id=1, source_target_pairs={{0,4},{1,3},{2,6},{3,1},{4,0},{5,7},{6,2},{7,5},{8,12},{9,11},{10,... | collective-permute-start | bytes 884744 | tf_op jit(solution)/shard_map/ppermute | solution.py:678
  58.1 9.9 %collective-permute-start.11 = (f32[528,128]{1,0:T(8,128)S(1)}, f32[528,128]{1,0:T(8,128)S(1)}, u32[]{:S(2)}, u32[]{:S(2)}) collective-permute-start(f32[528,128]{1,0:T(8,128)S(1)} %get-tuple-element.23), channel_id=1, source_target_pairs={{0,8},{8,16},{16,24},{1,9},{9,17},{17,25},{2,10},{10,18},{18,26},{... | collective-permute-start | bytes 811016 | tf_op jit(solution)/shard_map/ppermute | solution.py:636
  64.1 2.6 %collective-permute-start.12 = (f32[384,128]{1,0:T(8,128)S(1)}, f32[384,128]{1,0:T(8,128)S(1)}, u32[]{:S(2)}, u32[]{:S(2)}) collective-permute-start(f32[384,128]{1,0:T(8,128)S(1)} %get-tuple-element.24.mine_ref), channel_id=1, source_target_pairs={{0,1},{1,0},{2,3},{3,2},{4,5},{5,4},{6,7},{7,6},{8,9},{9,8},{10,11... | collective-permute-start | bytes 589832 | tf_op jit(solution)/shard_map/ppermute | solution.py:640
  64.2 1.6 %collective-permute-start.10 = (bf16[384,128]{1,0:T(8,128)(2,1)S(1)}, bf16[384,128]{1,0:T(8,128)(2,1)S(1)}, u32[]{:S(2)}, u32[]{:S(2)}) collective-permute-start(bf16[384,128]{1,0:T(8,128)(2,1)S(1)} %get-tuple-element.22.mine_ref), channel_id=1, source_target_pairs={{0,1},{1,0},{2,3},{3,2},{4,5},{5,4},{6,7},{7,6},{8,9},{9,8},{10,11... | collective-permute-start | bytes 294920 | tf_op jit(solution)/shard_map/ppermute | solution.py:640
